TPU v7x, 128 devices: a whole 4x4x4 slice. The times are simulated.
128 devices in a mesh: shell: 8 (over y_hi, x), order: 16 (over y_lo, z, core).
Axes of the slice: x: 4, y: 4 (y_hi: 2, y_lo: 2; y = y_hi * 2 + y_lo), z: 4, core: 2. Of those that a mesh axis runs over, the one named last changes fastest.
Arguments:
- velocity: bfloat16 [2, 2, 128, 128, 1024], P(None, None, 'order', 'shell'), may hold values from -6 to 6
- magnetic: bfloat16 [2, 2, 128, 128, 1024], P(None, None, 'order', 'shell'), may hold values from -6 to 6
- legendre: bfloat16 [128, 1024, 1536], P('order'), may hold values from -0.1875 to 0.1875
- quad_weight: float32 [1536], replicated, may hold values from 0.25 to 1.75
- order_table: int32 [128], replicated, may hold values from 0 to 1023, as said below
- field_prev: float32 [2, 128, 128, 1024], P(None, 'order', 'shell'), may hold values from -6 to 6
- rates: float32 [128], replicated, may hold values from 0.05 to 4
- radial_right: float32 [128, 128], replicated, may hold values from -0.5 to 0.5
- radial_left: float32 [128, 128], replicated, may hold values from -0.5 to 0.5
Outputs:
- field_next: float32 [2, 128, 128, 1024], P(None, 'order', 'shell')
Inputs may be any that keep to these rules, and one draw needn't show every extreme that they name: `order_table`: slots come in pairs: slot 2 i holds an order m and slot 2 i + 1 holds 1023 - m. All slots hold different orders, and the pair of 0 and 1023 is always present.
All inputs are finite; a program needn't handle non-finite values.
Results may differ from a plain program's by a relative error of at most 0.0058.
Values may be sent and summed in bfloat16 or wider, within the bound.
A program may use at most 128 MiB of HBM per device.

v0:
```python
import math

import jax
import jax.numpy as jnp
from jax import lax
from jax.sharding import PartitionSpec as P

NLON = 3072


def phase_pairs(order_table, lon_count):
    lon_index = jnp.arange(lon_count, dtype=jnp.int32)
    phase_index = order_table[:, None] * lon_index[None, :] % lon_count
    angles = phase_index.astype(jnp.float32) * (2.0 * math.pi / lon_count)
    return jnp.stack([jnp.cos(angles), -jnp.sin(angles)], 1).astype(jnp.bfloat16)


def grid_spectra(flattened, phases, row_weight):
    orders = flattened.shape[0]
    row_count = flattened.shape[3]
    block_size = math.gcd(row_count, 512)
    block_count = row_count // block_size
    synth_scale = 1.0 / math.sqrt(orders)
    lon_scale = 1.0 / math.sqrt(phases.shape[2])

    def one_block(block_index, output):
        first = block_index * block_size
        block_data = lax.dynamic_slice_in_dim(flattened, first, block_size, 3)
        block_weight = lax.dynamic_slice_in_dim(row_weight, first, block_size, 0)
        grid_vals = (
            jnp.einsum("sfkp,skj->fpj", block_data, phases, preferred_element_type=jnp.float32)
            * synth_scale
        )
        electromotive = (grid_vals[0] * grid_vals[3] - grid_vals[1] * grid_vals[2]).astype(
            jnp.bfloat16
        )
        spectra = jnp.einsum(
            "pj,skj->skp", electromotive, phases, preferred_element_type=jnp.float32
        )
        spectra = (spectra * lon_scale * block_weight[None, None, :]).astype(jnp.bfloat16)
        return lax.dynamic_update_slice_in_dim(output, spectra, first, 2)

    initial = jnp.zeros((orders, 2, row_count), jnp.bfloat16)
    return lax.fori_loop(0, block_count, one_block, initial)


def damping(rates, degrees, deg_total):
    return (
        1.0
        + rates[:, None]
        + 4.0 * degrees[None, :] * (degrees[None, :] + 1.0) / (deg_total * (deg_total - 1.0))
    )


def body(
    velocity,
    magnetic,
    legendre,
    quad_weight,
    order_table,
    field_prev,
    rates,
    radial_right,
    radial_left,
):
    coeffs = jnp.concatenate([velocity, magnetic], 0)
    synthesis = jnp.einsum(
        "fksrl,slt->sfkrt", coeffs, legendre, preferred_element_type=jnp.float32
    ).astype(jnp.bfloat16)
    orders = order_table.shape[0]
    deg_total = legendre.shape[1]
    phases = phase_pairs(order_table, NLON)
    exchanged = lax.all_to_all(synthesis, "order", split_axis=4, concat_axis=0, tiled=True)
    lat_band = exchanged.shape[4]
    first_row = lax.axis_index("order") * lat_band
    row_weight = jnp.tile(
        lax.dynamic_slice_in_dim(quad_weight, first_row, lat_band, 0), exchanged.shape[3]
    )
    flattened = exchanged.reshape(orders, 4, 2, exchanged.shape[3] * exchanged.shape[4])
    spectra = grid_spectra(flattened, phases, row_weight)
    spectra = spectra.reshape(orders, 2, exchanged.shape[3], exchanged.shape[4])
    returned = lax.all_to_all(spectra, "order", split_axis=0, concat_axis=3, tiled=True)
    analysed = jnp.einsum("skrt,slt->ksrl", returned, legendre, preferred_element_type=jnp.float32)
    rhs = field_prev + analysed
    owned_rows = lax.all_to_all(rhs, "shell", split_axis=3, concat_axis=2, tiled=True)
    deg_count = owned_rows.shape[3]
    deg_first = lax.axis_index("shell") * deg_count
    degrees = (deg_first + jnp.arange(deg_count, dtype=jnp.int32)).astype(jnp.float32)
    mixed_radii = jnp.einsum(
        "qr,ksrl->ksql", radial_right, owned_rows, precision=lax.Precision.HIGHEST
    )
    scaled = mixed_radii / damping(rates, degrees, deg_total)
    result = jnp.einsum("rq,ksql->ksrl", radial_left, scaled, precision=lax.Precision.HIGHEST)
    return lax.all_to_all(result, "shell", split_axis=2, concat_axis=3, tiled=True)


def solution(mesh):
    return jax.shard_map(
        body,
        mesh=mesh,
        in_specs=(
            P(None, None, "order", "shell", None),
            P(None, None, "order", "shell", None),
            P("order", None, None),
            P(),
            P(),
            P(None, "order", "shell", None),
            P(),
            P(),
            P(),
        ),
        out_specs=P(None, "order", "shell", None),
        check_vma=False,
    )
```

profile of v0, /device:TPU:0, one launch (start us, length us, event | category | flops | bytes accessed | tf_op | source)
XLA Modules:
  0.0 423.1 jit_solution(619970431294551137)
XLA Ops:
  0.0 12.3 %fusion.24 = bf16[8,4,2,16,1536]{4,3,2,1,0:T(8,128)(2,1)S(1)} fusion(bf16[8,1024,1536]{2,1,0:T(8,128)(2,1)} %param.13, bf16[2,2,8,16,1024]{4,3,2,1,0:T(8,128)(2,1)} %param.12, bf16[2,2,8,16,1024]{4,3,2,1,0:T(8,128)(2,1)} %param.11), kind=kOutput, calls=%fused_computation.19 | convolution fusion | flops 3223846912 | bytes 30408704 | tf_op jit(solution)/shard_map/fksrl,slt->sfkrt/dot_general | solution.py:67
  12.3 44.2 %copy.50 = bf16[8,4,2,16,1536]{3,2,1,0,4:T(2,128)(2,1)} copy(bf16[8,4,2,16,1536]{4,3,2,1,0:T(8,128)(2,1)S(1)} %fusion.24) | data formatting | bytes 6291456 | tf_op jit(solution)/shard_map/convert_element_type | solution.py:69
  56.5 27.8 %reshape.141 = bf16[16,2,49152]{2,1,0:T(2,128)(2,1)} reshape(bf16[1536,8,4,2,16]{4,3,2,1,0:T(2,128)(2,1)} %bitcast.98) | data formatting | bytes 6291456
  84.3 6.7 %all-to-all-start = ((bf16[16,2,49152]{2,1,0:T(2,128)(2,1)}), bf16[16,2,49152]{2,1,0:T(2,128)(2,1)}, u32[]{:S(2)}, u32[]{:S(2)}) async-start(bf16[16,2,49152]{2,1,0:T(2,128)(2,1)} %reshape.141), calls=%async_computation | async-start | bytes 6291456 | tf_op jit(solution)/shard_map/all_to_all | solution.py:73
  91.9 7.1 %cosine_convert_fusion = (bf16[128,1,3072]{2,0,1:T(8,128)(2,1)S(1)}, bf16[128,1,3072]{2,0,1:T(8,128)(2,1)S(1)}) fusion(s32[128]{0:T(128)S(1)} %copy-done.3), kind=kLoop, calls=%fused_computation.27 | loop fusion | flops 4718592 | bytes 1573376 | tf_op jit(solution)/shard_map/convert
  99.2 32.6 %all-to-all-done = bf16[16,2,49152]{2,1,0:T(2,128)(2,1)} async-done(((bf16[16,2,49152]{2,1,0:T(2,128)(2,1)}), bf16[16,2,49152]{2,1,0:T(2,128)(2,1)}, u32[]{:S(2)}, u32[]{:S(2)}) %all-to-all-start) | async-done | bytes 3145760 | tf_op jit(solution)/shard_map/all_to_all | solution.py:73
  131.7 20.3 %reshape.142 = bf16[1536,8,4,2,16]{4,3,2,1,0:T(2,128)(2,1)} reshape(bf16[16,2,49152]{2,1,0:T(2,128)(2,1)} %all-to-all-done) | data formatting | bytes 6291456
  152.0 58.3 %copy.51 = bf16[8,4,2,16,16,96]{5,3,0,4,2,1:T(8,128)(2,1)} copy(bf16[8,4,2,16,16,96]{3,2,1,0,5,4:T(2,128)(2,1)} %bitcast.99) | data formatting | bytes 6291456 | tf_op jit(solution)/shard_map/all_to_all | solution.py:73
  210.3 8.1 %reshape.132 = bf16[128,4,2,1536]{3,0,2,1:T(8,128)(2,1)} reshape(bf16[16,8,4,2,16,96]{5,4,1,0,3,2:T(8,128)(2,1)} %bitcast.102) | data formatting | bytes 6291456 | tf_op jit(solution)/shard_map/reshape | solution.py:79
  218.5 64.8 %while.13 = (s32[]{:T(128)}, bf16[128,2,1536]{0,2,1:T(8,128)(2,1)S(1)}, bf16[128,4,2,1536]{3,0,2,1:T(8,128)(2,1)}, bf16[128,2,3072]{2,0,1:T(8,128)(2,1)S(1)}, f3...) while((s32[]{:T(128)}, bf16[128,2,1536]{0,2,1:T(8,128)(2,1)S(1)}, ...), condition=%wide.region_1.2_spmd, body=%wide.region_0.1_spmd.sunk | while | flops 4039377408 | bytes 54794392 | solution.py:44
  218.5 11.5 %bitcast_multiply_fusion.2 = f32[4,512,3072]{2,1,0:T(8,128)} fusion(bf16[128,2,3072]{2,0,1:T(8,128)(2,1)S(1)} %get-tuple-element.186, bf16[128,4,2,1536]{3,0,2,1:T(8,128)(2,1)} %get-tuple-element.185, s32[]{:T(128)S(6)} %select_n.42), kind=kOutput, calls=%fused_computation.clone.1 | convolution fusion | flops 3227516928 | bytes 27787268 | tf_op jit(solution)/shard_map/while/body/eval_jaxpr/sfkp,skj->fpj/dot_general | solution.py:31
  230.0 10.0 %fusion.55 = bf16[128,2,1536]{0,2,1:T(8,128)(2,1)S(1)} fusion(bf16[128,2,1536]{0,2,1:T(8,128)(2,1)S(1)} %get-tuple-element.175, s32[]{:T(128)S(6)} %select_n.42, bf16[128,2,3072]{2,0,1:T(8,128)(2,1)S(1)} %get-tuple-element.186, f32[4,512,3072]{2,1,0:T(8,128)} %bitcast_multiply_fusion.2, f32[512]{0:T(512)S(1)} %dynamic-slice_multiply_fusion.2), kind=kOutput, calls=%fused_computation.11.clone.1 | convolution fusion | flops 811859968 | bytes 27002884 | tf_op jit(solution)/shard_map/while/body/eval_jaxpr/pj,skj->skp/dot_general | solution.py:37
  240.1 11.5 %bitcast_multiply_fusion.2 = f32[4,512,3072]{2,1,0:T(8,128)} fusion(bf16[128,2,3072]{2,0,1:T(8,128)(2,1)S(1)} %get-tuple-element.186, bf16[128,4,2,1536]{3,0,2,1:T(8,128)(2,1)} %get-tuple-element.185, s32[]{:T(128)S(6)} %select_n.42), kind=kOutput, calls=%fused_computation.clone.1 | convolution fusion | flops 3227516928 | bytes 27787268 | tf_op jit(solution)/shard_map/while/body/eval_jaxpr/sfkp,skj->fpj/dot_general | solution.py:31
  251.7 10.0 %fusion.55 = bf16[128,2,1536]{0,2,1:T(8,128)(2,1)S(1)} fusion(bf16[128,2,1536]{0,2,1:T(8,128)(2,1)S(1)} %get-tuple-element.175, s32[]{:T(128)S(6)} %select_n.42, bf16[128,2,3072]{2,0,1:T(8,128)(2,1)S(1)} %get-tuple-element.186, f32[4,512,3072]{2,1,0:T(8,128)} %bitcast_multiply_fusion.2, f32[512]{0:T(512)S(1)} %dynamic-slice_multiply_fusion.2), kind=kOutput, calls=%fused_computation.11.clone.1 | convolution fusion | flops 811859968 | bytes 27002884 | tf_op jit(solution)/shard_map/while/body/eval_jaxpr/pj,skj->skp/dot_general | solution.py:37
  261.7 11.5 %bitcast_multiply_fusion.2 = f32[4,512,3072]{2,1,0:T(8,128)} fusion(bf16[128,2,3072]{2,0,1:T(8,128)(2,1)S(1)} %get-tuple-element.186, bf16[128,4,2,1536]{3,0,2,1:T(8,128)(2,1)} %get-tuple-element.185, s32[]{:T(128)S(6)} %select_n.42), kind=kOutput, calls=%fused_computation.clone.1 | convolution fusion | flops 3227516928 | bytes 27787268 | tf_op jit(solution)/shard_map/while/body/eval_jaxpr/sfkp,skj->fpj/dot_general | solution.py:31
  273.3 10.0 %fusion.55 = bf16[128,2,1536]{0,2,1:T(8,128)(2,1)S(1)} fusion(bf16[128,2,1536]{0,2,1:T(8,128)(2,1)S(1)} %get-tuple-element.175, s32[]{:T(128)S(6)} %select_n.42, bf16[128,2,3072]{2,0,1:T(8,128)(2,1)S(1)} %get-tuple-element.186, f32[4,512,3072]{2,1,0:T(8,128)} %bitcast_multiply_fusion.2, f32[512]{0:T(512)S(1)} %dynamic-slice_multiply_fusion.2), kind=kOutput, calls=%fused_computation.11.clone.1 | convolution fusion | flops 811859968 | bytes 27002884 | tf_op jit(solution)/shard_map/while/body/eval_jaxpr/pj,skj->skp/dot_general | solution.py:37
  284.3 26.1 %all_to_all.69 = bf16[128,2,16,96]{3,2,1,0:T(8,128)(2,1)S(1)} all-to-all(bf16[128,2,16,96]{3,2,1,0:T(8,128)(2,1)S(1)} %copy.53), channel_id=1, replica_groups=mesh['shell'=8,'order'=16] {'order'}, dimensions={0} | all-to-all | bytes 1572864 | tf_op jit(solution)/shard_map/all_to_all | solution.py:82
  312.3 12.1 %fusion.37 = f32[2,8,16,1024]{3,2,0,1:T(8,128)S(1)} fusion(bf16[8,2,16,1536]{3,2,1,0:T(8,128)(2,1)S(1)} %all_to_all.56, bf16[8,1024,1536]{2,1,0:T(8,128)(2,1)} %param.13, f32[2,8,16,1024]{3,2,1,0:T(8,128)S(1)} %copy-done.1), kind=kOutput, calls=%fused_computation.36 | convolution fusion | flops 805568512 | bytes 28049408 | tf_op jit(solution)/shard_map/skrt,slt->ksrl/dot_general | solution.py:83
  324.4 8.6 %copy.56 = f32[2,8,16,1024]{2,0,1,3:T(2,128)} copy(f32[2,8,16,1024]{3,2,0,1:T(8,128)S(1)} %fusion.37) | data formatting | bytes 2097152 | tf_op jit(solution)/shard_map/add | solution.py:84
  333.0 13.6 %reshape.143 = f32[8,1,32768]{2,1,0:T(1,128)} reshape(f32[1024,8,2,16]{3,2,1,0:T(2,128)} %bitcast.100) | data formatting | bytes 2097152
  353.3 16.6 %all-to-all-done.2 = f32[8,1,32768]{2,1,0:T(1,128)S(1)} async-done(((f32[8,1,32768]{2,1,0:T(1,128)}), f32[8,1,32768]{2,1,0:T(1,128)S(1)}, u32[]{:S(2)}, u32[]{:S(2)}) %all-to-all-start.2) | async-done | bytes 1048608 | tf_op jit(solution)/shard_map/all_to_all | solution.py:85
  373.6 14.2 %reshape.144 = f32[1024,8,2,16]{3,2,1,0:T(2,128)} reshape(f32[8,32768]{1,0:T(8,128)S(1)} %reduce) | data formatting | bytes 2097152
  387.8 10.4 %copy.71 = f32[2,8,16,8,128]{4,2,3,1,0:T(8,128)S(1)} copy(f32[2,8,16,8,128]{2,0,1,4,3:T(2,128)} %bitcast.101) | data formatting | bytes 2097152 | tf_op jit(solution)/shard_map/all_to_all | solution.py:85
  401.6 19.7 %all_to_all.70 = f32[2,8,128,128]{3,1,0,2:T(8,128)S(1)} all-to-all(f32[2,8,128,128]{3,1,0,2:T(8,128)S(1)} %copy.60), channel_id=1, replica_groups=mesh['shell'=8,'order'=16] {'shell'}, dimensions={2} | all-to-all | bytes 2097152 | tf_op jit(solution)/shard_map/all_to_all | solution.py:94
  (31 shorter events, 19.6 us)
Async XLA Ops:
  0.0 398.3 %copy-start = (f32[128,128]{1,0:T(8,128)S(1)}, f32[128,128]{1,0:T(8,128)}, u32[]{:S(2)}) copy-start(f32[128,128]{1,0:T(8,128)} %param.18) | copy-start | bytes 196612
  84.3 7.6 %copy-start.3 = (s32[128]{0:T(128)S(1)}, s32[128]{0:T(128)}, u32[]{:S(2)}) copy-start(s32[128]{0:T(128)} %param.15) | copy-start | bytes 1540
  84.3 47.5 %all-to-all-start = ((bf16[16,2,49152]{2,1,0:T(2,128)(2,1)}), bf16[16,2,49152]{2,1,0:T(2,128)(2,1)}, u32[]{:S(2)}, u32[]{:S(2)}) async-start(bf16[16,2,49152]{2,1,0:T(2,128)(2,1)} %reshape.141), calls=%async_computation | async-start | bytes 6291456 | tf_op jit(solution)/shard_map/all_to_all | solution.py:73
  284.3 28.0 %copy-start.1 = (f32[2,8,16,1024]{3,2,1,0:T(8,128)S(1)}, f32[2,8,16,1024]{3,2,1,0:T(8,128)}, u32[]{:S(2)}) copy-start(f32[2,8,16,1024]{3,2,1,0:T(8,128)} %param.16) | copy-start | bytes 3145732
  333.0 20.2 %copy-start.4 = (f32[128]{0:T(128)S(1)}, f32[128]{0:T(128)}, u32[]{:S(2)}) copy-start(f32[128]{0:T(128)} %param.17) | copy-start | bytes 1540
  346.6 23.4 %all-to-all-start.2 = ((f32[8,1,32768]{2,1,0:T(1,128)}), f32[8,1,32768]{2,1,0:T(1,128)S(1)}, u32[]{:S(2)}, u32[]{:S(2)}) async-start(f32[8,1,32768]{2,1,0:T(1,128)} %reshape.143), calls=%async_computation.2 | async-start | bytes 2097152 | tf_op jit(solution)/shard_map/all_to_all | solution.py:85
  398.2 1.8 copy-start.2
where the time goes:
time: 426 us; the launch traced here: 423 us
  local copies, waits for them, and re-layouts  212 us (50%)
  matrix products  91.7 us (22%)
  waiting for transfers between devices  49.2 us (12%)
  blocking collectives  45.9 us (11%)
  starting transfers between devices  13.3 us (3%)
  other arithmetic  10.7 us (3%)
    unnamed x14, local copies, waits for them, and re-layouts  75.8 us
    all_to_all x1, local copies, waits for them, and re-layouts, body(): lax.all_to_all(synthesis, 'order', split_axis=4, concat_axis=0, tiled=True)  58.3 us
    convert_element_type x1, local copies, waits for them, and re-layouts, body(): synthesis = jnp.einsum('fksrl,slt->sfkrt', coeffs, legendre, preferred_el...  44.2 us
    dot_general x3, matrix products, one_block(): jnp.einsum('sfkp,skj->fpj', block_data, phases, preferred_element_type=jn...  34.5 us
    all_to_all x1, waiting for transfers between devices, body(): lax.all_to_all(synthesis, 'order', split_axis=4, concat_axis=0, tiled=True)  32.6 us
    dot_general x3, matrix products, one_block(): jnp.einsum('pj,skj->skp', electromotive, phases, preferred_element_type=j...  30.1 us
    all_to_all x1, blocking collectives, body(): lax.all_to_all(spectra, 'order', split_axis=0, concat_axis=3, tiled=True)  26.1 us
    all_to_all x1, blocking collectives, body(): lax.all_to_all(result, 'shell', split_axis=2, concat_axis=3, tiled=True)  19.7 us
  transfers between devices with their start and end apart: 2, of which 2 were waited for; matrix products, arithmetic and copies ran while one was open for 2% of the time, Pallas kernels for 0%

commit v1 on v0

v1 whole, which is shorter than its diff:
```python
import functools
import math

import jax
import jax.numpy as jnp
from jax import lax
from jax.experimental import pallas as pl
from jax.experimental.pallas import tpu as pltpu
from jax.sharding import PartitionSpec as P

NLON = 3072
NLAT = 1536
NDEG = 1024
NO = 16
NH = 8
SL = 8
RL = 16
KK = 256
TC = 256
NC = NLAT // TC
JT = 512
GS = 2
NG = SL // GS
GR = GS * 32
BF = jnp.bfloat16
F32 = jnp.float32
STEP = 2.0 * math.pi / NLON


def iota(shape, dim):
    return lax.broadcasted_iota(jnp.int32, shape, dim)


def angle(order, position):
    return ((order * position) % NLON).astype(F32) * STEP


def kernel(
    vel, mag, leg, qw, ot, fprev, rates, right, left, out,
    xv, xm, lv, ybuf, perm, perm_t, ph_t, ph_m, sbuf, rbuf, emf, spec_s, spec_r, acc,
    rhs_s, rhs_r, res_s, res_r, invden,
    x_sem, l_sem, f_sem, own_sem, s1, r1, own2_sem, s2, r2, own3_sem, s3, r3, own4_sem, s4, r4,
):
    me = lax.axis_index("order")
    mh = lax.axis_index("shell")

    def leg_copy(c):
        return pltpu.make_async_copy(
            leg.at[:, :, pl.ds(pl.multiple_of(c * TC, TC), TC)], lv.at[c], l_sem.at[c]
        )

    copy_v = pltpu.make_async_copy(vel, xv, x_sem.at[0])
    copy_m = pltpu.make_async_copy(mag, xm, x_sem.at[1])
    copy_f = [
        pltpu.make_async_copy(fprev.at[k], acc.at[:, pl.ds(16 * k, 16), :], f_sem.at[k])
        for k in range(2)
    ]
    copy_v.start()
    copy_m.start()
    for c in range(NC):
        leg_copy(c).start()
    for k in range(2):
        copy_f[k].start()

    barrier = pltpu.get_barrier_semaphore()

    @pl.loop(1, NO)
    def _(i):
        pl.semaphore_signal(
            barrier, inc=1, device_id=(mh, (me + i) % NO), device_id_type=pl.DeviceIdType.MESH
        )

    @pl.loop(1, NH)
    def _(i):
        pl.semaphore_signal(
            barrier, inc=1, device_id=((mh + i) % NH, me), device_id_type=pl.DeviceIdType.MESH
        )

    row, col = iota((KK, KK), 0), iota((KK, KK), 1)
    source = (row % 8) * 32 + ((row // 8) % 2) * 16 + row // 16
    perm[...] = (col == source).astype(F32).astype(BF)
    source_t = (col % 8) * 32 + ((col // 8) % 2) * 16 + col // 16
    perm_t[...] = (row == source_t).astype(F32).astype(BF)

    copy_v.wait()
    copy_m.wait()
    pl.semaphore_wait(barrier, NO + NH - 2)

    def fields_copy(c, dest):
        return pltpu.make_async_remote_copy(
            src_ref=sbuf.at[c, :, dest],
            dst_ref=rbuf.at[c, :, me],
            send_sem=s1.at[c],
            recv_sem=r1.at[c],
            device_id=(mh, dest),
            device_id_type=pl.DeviceIdType.MESH,
        )

    def own_fields(c):
        return pltpu.make_async_copy(sbuf.at[c, :, me], rbuf.at[c, :, me], own_sem.at[c])

    @pl.loop(0, NC)
    def _(c):
        leg_copy(c).wait()

        @pl.loop(0, SL)
        def _(s):
            x = jnp.concatenate(
                [xv[:, s].reshape(64, NDEG), xm[:, s].reshape(64, NDEG)], axis=0
            )
            y = jnp.dot(x, lv[c, s], preferred_element_type=F32).astype(BF)
            first = pl.multiple_of(s * 32, 32)
            for f in range(4):
                ybuf[f, pl.ds(first, 32), :] = y[32 * f : 32 * f + 32]

        for f in range(4):
            z = jnp.dot(perm[...], ybuf[f], preferred_element_type=F32).astype(BF)
            sbuf[c, f] = z.reshape(NO, 16, TC)

        @pl.loop(1, NO)
        def _(i):
            fields_copy(c, (me + i) % NO).start()

        own_fields(c).start()

    orders = ot[...]
    r0, c0 = iota((KK, 128), 0), iota((KK, 128), 1)
    hit = c0 == (r0 // 16) * 8 + r0 % 8
    order_col = jnp.sum(jnp.where(hit, orders.astype(F32), 0.0), axis=1, keepdims=True)
    order_col = order_col.astype(jnp.int32)
    odd = (r0 // 8) % 2 == 1
    fine = angle(order_col, c0)
    cb, sb = jnp.cos(fine), jnp.sin(fine)
    dm = jnp.where(odd, -sb, cb)
    em = jnp.where(odd, -cb, -sb)
    coarse = angle(order_col, (c0 % (NLON // 128)) * 128)
    ca, sa = jnp.cos(coarse), jnp.sin(coarse)
    for a in range(NLON // 128):
        ph_m[:, a * 128 : a * 128 + 128] = (ca[:, a : a + 1] * dm + sa[:, a : a + 1] * em).astype(BF)

    r1_, c1_ = iota((128, 128), 0), iota((128, 128), 1)
    slot_col = jnp.sum(jnp.where(r1_ == c1_, orders.astype(F32), 0.0), axis=1, keepdims=True)
    r2_, c2_ = iota((128, KK), 0), iota((128, KK), 1)
    hit_t = r2_ == (c2_ // 16) * 8 + c2_ % 8
    order_row = jnp.sum(jnp.where(hit_t, slot_col, 0.0), axis=0, keepdims=True).astype(jnp.int32)
    r3_, c3_ = iota((64, KK), 0), iota((64, KK), 1)
    odd_t = (c3_ // 8) % 2 == 1
    fine_t = angle(order_row, r3_)
    cbt, sbt = jnp.cos(fine_t), jnp.sin(fine_t)
    dt = jnp.where(odd_t, -sbt, cbt)
    et = jnp.where(odd_t, -cbt, -sbt)
    coarse_t = angle(order_row, iota((NLON // 64, KK), 0) * 64)
    cat, sat = jnp.cos(coarse_t), jnp.sin(coarse_t)
    for a in range(NLON // 64):
        ph_t[a * 64 : a * 64 + 64, :] = (cat[a : a + 1] * dt + sat[a : a + 1] * et).astype(BF)

    rate_col = jnp.sum(jnp.where(r1_ == c1_, rates[...], 0.0), axis=1, keepdims=True)
    degree = (mh * 128 + c1_).astype(F32)
    invden[...] = 1.0 / (1.0 + rate_col + 4.0 * degree * (degree + 1.0) / (NDEG * (NDEG - 1.0)))

    scale = 1.0 / (128.0 * math.sqrt(NLON))

    def spectra_copy(c, dest):
        return pltpu.make_async_remote_copy(
            src_ref=spec_s.at[c, dest],
            dst_ref=spec_r.at[c, me],
            send_sem=s2.at[c],
            recv_sem=r2.at[c],
            device_id=(mh, dest),
            device_id_type=pl.DeviceIdType.MESH,
        )

    def own_spectra(c):
        return pltpu.make_async_copy(spec_s.at[c, me], spec_r.at[c, me], own2_sem.at[c])

    def grid_chunk(c):
        own_fields(c).wait()
        several = rbuf.at[c, :, pl.ds(0, NO - 1)]
        pltpu.make_async_copy(several, several, r1.at[c]).wait()

        @pl.loop(0, NLON // JT)
        def _(j):
            rows = pl.ds(pl.multiple_of(j * JT, JT), JT)
            ph = ph_t[rows, :]
            g = [
                jnp.dot(ph, rbuf[c, f].reshape(KK, TC), preferred_element_type=F32)
                for f in range(4)
            ]
            emf[rows, :] = (g[0] * g[3] - g[1] * g[2]).astype(BF)

        spec = jnp.dot(ph_m[...], emf[...], preferred_element_type=F32)
        weight = qw[:, pl.ds(pl.multiple_of(c * TC, TC), TC)] * scale
        spec_s[c] = (spec * weight).astype(BF).reshape(NO, 16, TC)

        @pl.loop(1, NO)
        def _(i):
            spectra_copy(c, (me + i) % NO).start()

        own_spectra(c).start()

    def spectra_rows(c):
        own_spectra(c).wait()
        several = spec_r.at[c, pl.ds(0, NO - 1)]
        pltpu.make_async_copy(several, several, r2.at[c]).wait()
        z = jnp.dot(perm_t[...], spec_r[c].reshape(KK, TC), preferred_element_type=F32)
        ybuf[0] = z.astype(BF)

    def analyse_slot(c, s):
        part = lax.dot_general(
            ybuf[0, pl.ds(pl.multiple_of(s * 32, 32), 32), :],
            lv[c, s],
            (((1,), (1,)), ((), ())),
            preferred_element_type=F32,
        )
        total = acc[s] + part
        acc[s] = total
        return total

    for k in range(2):
        copy_f[k].wait()

    grid_chunk(0)

    @pl.loop(1, NC)
    def _(c):
        grid_chunk(c)
        spectra_rows(c - 1)

        @pl.loop(0, SL)
        def _(s):
            analyse_slot(c - 1, s)

    spectra_rows(NC - 1)

    def rhs_copy(g, dest):
        return pltpu.make_async_remote_copy(
            src_ref=rhs_s.at[g, dest],
            dst_ref=rhs_r.at[g, mh],
            send_sem=s3.at[g],
            recv_sem=r3.at[g],
            device_id=(dest, me),
            device_id_type=pl.DeviceIdType.MESH,
        )

    def own_rhs(g):
        return pltpu.make_async_copy(rhs_s.at[g, mh], rhs_r.at[g, mh], own3_sem.at[g])

    def result_copy(g, dest):
        return pltpu.make_async_remote_copy(
            src_ref=res_s.at[g, dest],
            dst_ref=res_r.at[g, mh],
            send_sem=s4.at[g],
            recv_sem=r4.at[g],
            device_id=(dest, me),
            device_id_type=pl.DeviceIdType.MESH,
        )

    def own_result(g):
        return pltpu.make_async_copy(res_s.at[g, mh], res_r.at[g, mh], own4_sem.at[g])

    @pl.loop(0, NG)
    def _(g):
        @pl.loop(0, GS)
        def _(i):
            total = analyse_slot(NC - 1, g * GS + i).astype(BF)
            rows = pl.ds(pl.multiple_of(i * 32, 32), 32)
            for d in range(NH):
                rhs_s[g, d, rows, :] = total[:, d * 128 : d * 128 + 128]

        @pl.loop(1, NH)
        def _(i):
            rhs_copy(g, (mh + i) % NH).start()

        own_rhs(g).start()

    @pl.loop(0, NG)
    def _(g):
        own_rhs(g).wait()
        several = rhs_r.at[g, pl.ds(0, NH - 1)]
        pltpu.make_async_copy(several, several, r3.at[g]).wait()
        x = jnp.concatenate(
            [rhs_r[g, :, 16 * b : 16 * b + 16, :].reshape(128, 128) for b in range(2 * GS)], axis=1
        ).astype(F32)
        mixed = jnp.dot(right[...], x, precision=lax.Precision.HIGHEST, preferred_element_type=F32)
        scaled = mixed * jnp.concatenate([invden[...]] * (2 * GS), axis=1)
        res = jnp.dot(left[...], scaled, precision=lax.Precision.HIGHEST, preferred_element_type=F32)
        res = res.astype(BF)
        for b in range(2 * GS):
            res_s[g, :, 16 * b : 16 * b + 16, :] = res[:, 128 * b : 128 * b + 128].reshape(8, 16, 128)

        @pl.loop(1, NH)
        def _(i):
            result_copy(g, (mh + i) % NH).start()

        own_result(g).start()

    @pl.loop(0, NG)
    def _(g):
        own_result(g).wait()
        several = res_r.at[g, pl.ds(0, NH - 1)]
        pltpu.make_async_copy(several, several, r4.at[g]).wait()
        for i in range(GS):
            for k in range(2):
                for d in range(NH):
                    out[k, g * GS + i, :, d * 128 : d * 128 + 128] = res_r[
                        g, d, (2 * i + k) * 16 : (2 * i + k) * 16 + 16, :
                    ].astype(F32)

    @pl.loop(0, NC)
    def _(c):
        several = sbuf.at[c, :, pl.ds(0, NO - 1)]
        pltpu.make_async_copy(several, several, s1.at[c]).wait()
        several = spec_s.at[c, pl.ds(0, NO - 1)]
        pltpu.make_async_copy(several, several, s2.at[c]).wait()

    @pl.loop(0, NG)
    def _(g):
        several = rhs_s.at[g, pl.ds(0, NH - 1)]
        pltpu.make_async_copy(several, several, s3.at[g]).wait()
        several = res_s.at[g, pl.ds(0, NH - 1)]
        pltpu.make_async_copy(several, several, s4.at[g]).wait()


def body(
    velocity, magnetic, legendre, quad_weight, order_table, field_prev, rates, radial_right, radial_left
):
    hbm = pl.BlockSpec(memory_space=pl.ANY)
    vmem = pl.BlockSpec(memory_space=pltpu.VMEM)
    sem = pltpu.SemaphoreType.DMA
    return pl.pallas_call(
        kernel,
        out_shape=jax.ShapeDtypeStruct((2, SL, RL, NDEG), F32),
        in_specs=[hbm, hbm, hbm, vmem, vmem, hbm, vmem, vmem, vmem],
        out_specs=vmem,
        scratch_shapes=[
            pltpu.VMEM((4, SL, RL, NDEG), BF),
            pltpu.VMEM((4, SL, RL, NDEG), BF),
            pltpu.VMEM((NC, SL, NDEG, TC), BF),
            pltpu.VMEM((4, KK, TC), BF),
            pltpu.VMEM((KK, KK), BF),
            pltpu.VMEM((KK, KK), BF),
            pltpu.VMEM((NLON, KK), BF),
            pltpu.VMEM((KK, NLON), BF),
            pltpu.VMEM((NC, 4, NO, 16, TC), BF),
            pltpu.VMEM((NC, 4, NO, 16, TC), BF),
            pltpu.VMEM((NLON, TC), BF),
            pltpu.VMEM((NC, NO, 16, TC), BF),
            pltpu.VMEM((NC, NO, 16, TC), BF),
            pltpu.VMEM((SL, 32, NDEG), F32),
            pltpu.VMEM((NG, NH, GR, 128), BF),
            pltpu.VMEM((NG, NH, GR, 128), BF),
            pltpu.VMEM((NG, NH, GR, 128), BF),
            pltpu.VMEM((NG, NH, GR, 128), BF),
            pltpu.VMEM((128, 128), F32),
            sem((2,)),
            sem((NC,)),
            sem((2,)),
            sem((NC,)),
            sem((NC,)),
            sem((NC,)),
            sem((NC,)),
            sem((NC,)),
            sem((NC,)),
            sem((NG,)),
            sem((NG,)),
            sem((NG,)),
            sem((NG,)),
            sem((NG,)),
            sem((NG,)),
        ],
        compiler_params=pltpu.CompilerParams(
            collective_id=0, has_side_effects=True, vmem_limit_bytes=58 * 1024 * 1024
        ),
        cost_estimate=pl.CostEstimate(
            flops=18_000_000_000, bytes_accessed=32_000_000, transcendentals=0
        ),
    )(
        velocity.reshape(4, SL, RL, NDEG),
        magnetic.reshape(4, SL, RL, NDEG),
        legendre,
        quad_weight.reshape(1, NLAT),
        order_table.reshape(1, 128),
        field_prev,
        rates.reshape(1, 128),
        radial_right,
        radial_left,
    )


def solution(mesh):
    return jax.shard_map(
        body,
        mesh=mesh,
        in_specs=(
            P(None, None, "order", "shell", None),
            P(None, None, "order", "shell", None),
            P("order", None, None),
            P(),
            P(),
            P(None, "order", "shell", None),
            P(),
            P(),
            P(),
        ),
        out_specs=P(None, "order", "shell", None),
        check_vma=False,
    )
```

time: 426 us -> 103 us (0.24)
  local copies, waits for them, and re-layouts: 212 us -> 3.6 us
  Pallas kernels: 0 us -> 98.9 us
  matrix products: 91.7 us -> 0 us
  waiting for transfers between devices: 49.2 us -> 0 us
  blocking collectives: 45.9 us -> 0 us
  starting transfers between devices: 13.3 us -> 0 us
  other arithmetic: 10.7 us -> 0 us
    pallas_call x0 -> x1, Pallas kernels: none -> 98.9 us  [body(): pl.pallas_call(kernel, out_shape=jax.ShapeDtypeStruct((2, SL, RL, NDEG),...]
    dot_general x10 -> x0, matrix products: 91.7 us -> none  [the longest x3 34.5 us: one_block(): jnp.einsum('sfkp,skj->fpj', block_data, phases, preferred_element_type=jn...]
    unnamed x14 -> x1, local copies, waits for them, and re-layouts: 75.8 us -> 2.31 us
    all_to_all x7 -> x0, local copies, waits for them, and re-layouts: 72.9 us -> none  [the longest x1 58.3 us: body(): lax.all_to_all(synthesis, 'order', split_axis=4, concat_axis=0, tiled=True)]
    all_to_all x2 -> x0, waiting for transfers between devices: 49.2 us -> none  [the longest x1 32.6 us: body(): lax.all_to_all(synthesis, 'order', split_axis=4, concat_axis=0, tiled=True)]
    all_to_all x2 -> x0, blocking collectives: 45.9 us -> none  [the longest x1 26.1 us: body(): lax.all_to_all(spectra, 'order', split_axis=0, concat_axis=3, tiled=True)]
    convert_element_type x1 -> x0, local copies, waits for them, and re-layouts: 44.2 us -> none  [body(): synthesis = jnp.einsum('fksrl,slt->sfkrt', coeffs, legendre, preferred_el...]
    all_to_all x2 -> x0, starting transfers between devices: 13.3 us -> none  [the longest x1 6.7 us: body(): lax.all_to_all(synthesis, 'order', split_axis=4, concat_axis=0, tiled=True)]
  transfers between devices with their start and end apart: 2 -> 0, of which waited for: 2 -> 0; matrix products, arithmetic and copies ran while one was open for 2% -> 0% of each run, Pallas kernels for 0% -> 0%
where the time goes in v1:
time: 103 us; the launch traced here: 102 us
  Pallas kernels  98.9 us (96%)
  local copies, waits for them, and re-layouts  3.6 us (3%)
    pallas_call x1, Pallas kernels, body(): pl.pallas_call(kernel, out_shape=jax.ShapeDtypeStruct((2, SL, RL, NDEG),...  98.9 us
    unnamed x1, local copies, waits for them, and re-layouts  2.31 us

profile of v1, /device:TPU:0, one launch (start us, length us, event | category | flops | bytes accessed | tf_op | source)
XLA Modules:
  0.0 102.5 jit_solution(11836224788291006635)
XLA Ops:
  0.0 1.3 %reshape.17.qw = f32[1,1536]{1,0:T(1,128)} reshape(f32[1536]{0:T(1024)} %param.12) | data formatting | bytes 12288 | tf_op jit(solution)/shard_map/reshape | solution.py:381
  1.3 98.9 %shard_map.91 = f32[2,8,16,1024]{3,2,1,0:T(8,128)} custom-call(bf16[4,8,16,1024]{3,2,1,0:T(8,128)(2,1)} %bitcast.4, bf16[4,8,16,1024]{3,2,1,0:T(8,128)(2,1)} %bitcast.5, bf16[8,1024,1536]{2,1,0:T(8,128)(2,1)} %leg.1, f32[1,1536]{1,0:T(1,128)} %reshape.17.qw, s32[1,128]{1,0:T(1,128)} %bitcast.6, f32[2,8,16,1024]{3,2,1,0:T(8,128)} %fprev.1, f32[1,128]{1,0:T(1,128)} %bitcast.7, ...), custom_call_target="tpu_custom_call" | custom-call | flops 17999998976 | bytes 32000000 | tf_op jit(solution)/shard_map/pallas_call | solution.py:330
  100.2 2.3 %copy.11 = f32[2,8,16,1024]{3,2,1,0:T(8,128)} copy(f32[2,8,16,1024]{3,2,1,0:T(8,128)} %shard_map.91) | data formatting | bytes 2097152

commit v2 on v1

v2 whole, which is shorter than its diff:
```python
import math

import jax
import jax.numpy as jnp
from jax import lax
from jax.experimental import pallas as pl
from jax.experimental.pallas import tpu as pltpu
from jax.sharding import PartitionSpec as P

NLON = 3072
NLAT = 1536
NDEG = 1024
NO = 16
NX = 4
NH = 8
SL = 8
RL = 16
KK = 256
TC = 256
NC = NLAT // TC
JT = 512
LB = 256
NB = NDEG // LB
NP = 2 * NO
BF = jnp.bfloat16
F32 = jnp.float32
STEP = 2.0 * math.pi / NLON
MESH = pl.DeviceIdType.MESH


def iota(shape, dim):
    return lax.broadcasted_iota(jnp.int32, shape, dim)


def angle(order, position):
    return ((order * position) % NLON).astype(F32) * STEP


def slot_of(q):
    return ((q % 16) // 8) * 4 + q % 4


def part_of(q):
    return (q // 4) % 2


def split(x):
    high = x.astype(BF)
    return high, (x - high.astype(F32)).astype(BF)


def all_but_one(ref, sem):
    pltpu.make_async_copy(ref, ref, sem).wait()


def kernel(
    vel, mag, leg, qw, ot, fprev, rates, right, left, out,
    xv, xm, lv, fp, fp_s, fp_r, ybuf, perm, perm2, ph_t, ph_m, sbuf, rbuf, emf, spec_s, spec_r,
    fwd_s, fwd_r, acc, res_s, invden, right_c, left_c,
    x_sem, l_sem, f_sem, o0, s0, r0, o1, s1, r1, o2, s2, r2, o3, s3, r3, o4, s4, r4,
):
    me = lax.axis_index("order")
    mh = lax.axis_index("shell")
    my = mh // NX
    mx = mh % NX
    mp = my * NO + me

    def leg_copy(c, s):
        return pltpu.make_async_copy(
            leg.at[s, :, pl.ds(pl.multiple_of(c * TC, TC), TC)], lv.at[c, s], l_sem.at[c, s]
        )

    copy_v = pltpu.make_async_copy(vel, xv, x_sem.at[0])
    copy_m = pltpu.make_async_copy(mag, xm, x_sem.at[1])
    copy_f = pltpu.make_async_copy(fprev, fp, f_sem)
    copy_f.start()
    copy_v.start()
    copy_m.start()

    @pl.loop(0, NC)
    def _(c):
        @pl.loop(0, SL)
        def _(s):
            leg_copy(c, s).start()

    barrier = pltpu.get_barrier_semaphore()

    @pl.loop(1, NP)
    def _(i):
        p = (mp + i) % NP
        pl.semaphore_signal(
            barrier, inc=1, device_id=((p // NO) * NX + mx, p % NO), device_id_type=MESH
        )

    @pl.loop(1, NX)
    def _(i):
        x = (mx + i) % NX
        for y in range(2):
            pl.semaphore_signal(barrier, inc=1, device_id=(y * NX + x, me), device_id_type=MESH)

    row, col = iota((KK, KK), 0), iota((KK, KK), 1)
    source = slot_of(row) * 32 + part_of(row) * 16 + row // 16
    perm[...] = (col == source).astype(F32).astype(BF)
    row, col = iota((512, 512), 0), iota((512, 512), 1)
    source = (row % 32) * 16 + (row // 256) * 8 + ((row // 32) % 2) * 4 + (row % 256) // 64
    perm2[...] = (col == source).astype(F32).astype(BF)

    def prev_copy(dest):
        return pltpu.make_async_remote_copy(
            src_ref=fp_s.at[dest], dst_ref=fp_r.at[mh], send_sem=s0, recv_sem=r0,
            device_id=(dest, me), device_id_type=MESH,
        )

    own_prev = pltpu.make_async_copy(fp_s.at[mh], fp_r.at[mh], o0)
    copy_f.wait()
    for k in range(2):
        fp_s[:, 16 * k : 16 * k + 16, :] = fp[k].astype(BF)
    pl.semaphore_wait(barrier, NP - 1 + 2 * (NX - 1))

    @pl.loop(1, NH)
    def _(i):
        prev_copy((mh + i) % NH).start()

    own_prev.start()
    copy_v.wait()
    copy_m.wait()

    def fields_copy(c, dest):
        return pltpu.make_async_remote_copy(
            src_ref=sbuf.at[c, :, dest], dst_ref=rbuf.at[c, :, me],
            send_sem=s1.at[c], recv_sem=r1.at[c],
            device_id=(mh, dest), device_id_type=MESH,
        )

    def own_fields(c):
        return pltpu.make_async_copy(sbuf.at[c, :, me], rbuf.at[c, :, me], o1.at[c])

    @pl.loop(0, NC)
    def _(c):
        @pl.loop(0, SL)
        def _(s):
            leg_copy(c, s).wait()
            x = jnp.concatenate(
                [xv[:, s].reshape(64, NDEG), xm[:, s].reshape(64, NDEG)], axis=0
            )
            y = jnp.dot(x, lv[c, s], preferred_element_type=F32).astype(BF)
            first = pl.multiple_of(s * 32, 32)
            for f in range(4):
                ybuf[f, pl.ds(first, 32), :] = y[32 * f : 32 * f + 32]

        for f in range(4):
            z = jnp.dot(perm[...], ybuf[f], preferred_element_type=F32).astype(BF)
            sbuf[c, f] = z.reshape(NO, 16, TC)

        @pl.loop(1, NO)
        def _(i):
            fields_copy(c, (me + i) % NO).start()

        own_fields(c).start()

    orders = ot[...].astype(F32)
    ra, ca = iota((KK, 128), 0), iota((KK, 128), 1)
    hit = ca == (ra // 16) * 8 + slot_of(ra)
    order_col = jnp.sum(jnp.where(hit, orders, 0.0), axis=1, keepdims=True).astype(jnp.int32)
    odd = part_of(ra) == 1
    fine = angle(order_col, ca)
    cb, sb = jnp.cos(fine), jnp.sin(fine)
    dm = jnp.where(odd, -sb, cb)
    em = jnp.where(odd, -cb, -sb)
    coarse = angle(order_col, (ca % (NLON // 128)) * 128)
    cc, sc = jnp.cos(coarse), jnp.sin(coarse)
    for a in range(NLON // 128):
        ph_m[:, a * 128 : a * 128 + 128] = (cc[:, a : a + 1] * dm + sc[:, a : a + 1] * em).astype(BF)

    rb, cb2 = iota((128, 128), 0), iota((128, 128), 1)
    slot_col = jnp.sum(jnp.where(rb == cb2, orders, 0.0), axis=1, keepdims=True)
    rd, cd = iota((128, KK), 0), iota((128, KK), 1)
    hit_t = rd == (cd // 16) * 8 + slot_of(cd)
    order_row = jnp.sum(jnp.where(hit_t, slot_col, 0.0), axis=0, keepdims=True).astype(jnp.int32)
    re, ce = iota((64, KK), 0), iota((64, KK), 1)
    odd_t = part_of(ce) == 1
    fine_t = angle(order_row, re)
    cbt, sbt = jnp.cos(fine_t), jnp.sin(fine_t)
    dt = jnp.where(odd_t, -sbt, cbt)
    et = jnp.where(odd_t, -cbt, -sbt)
    coarse_t = angle(order_row, iota((NLON // 64, KK), 0) * 64)
    cat, sat = jnp.cos(coarse_t), jnp.sin(coarse_t)
    for a in range(NLON // 64):
        ph_t[a * 64 : a * 64 + 64, :] = (cat[a : a + 1] * dt + sat[a : a + 1] * et).astype(BF)

    rate_col = jnp.sum(jnp.where(rb == cb2, rates[...], 0.0), axis=1, keepdims=True)
    degree = iota((128, NDEG), 1).astype(F32)
    invden[...] = 1.0 / (1.0 + rate_col + 4.0 * degree * (degree + 1.0) / (NDEG * (NDEG - 1.0)))
    for factor, halves in ((right, right_c), (left, left_c)):
        high, low = split(factor[...])
        halves[...] = jnp.concatenate([high, low, high], axis=1)

    scale = 1.0 / (128.0 * math.sqrt(NLON))

    def spectra_copy(c, p):
        return pltpu.make_async_remote_copy(
            src_ref=spec_s.at[c, p % NO, p // NO], dst_ref=spec_r.at[c, mp],
            send_sem=s2.at[c], recv_sem=r2.at[c],
            device_id=((p // NO) * NX + mx, p % NO), device_id_type=MESH,
        )

    def own_spectra(c):
        return pltpu.make_async_copy(spec_s.at[c, me, my], spec_r.at[c, mp], o2.at[c])

    @pl.loop(0, NC)
    def _(c):
        own_fields(c).wait()
        all_but_one(rbuf.at[c, :, pl.ds(0, NO - 1)], r1.at[c])

        @pl.loop(0, NLON // JT)
        def _(j):
            rows = pl.ds(pl.multiple_of(j * JT, JT), JT)
            ph = ph_t[rows, :]
            g = [
                jnp.dot(ph, rbuf[c, f].reshape(KK, TC), preferred_element_type=F32)
                for f in range(4)
            ]
            emf[rows, :] = (g[0] * g[3] - g[1] * g[2]).astype(BF)

        spec = jnp.dot(ph_m[...], emf[...], preferred_element_type=F32)
        halves = []
        for th in range(2):
            weight = qw[pl.ds(2 * c + th, 1), :] * scale
            halves.append((spec[:, 128 * th : 128 * th + 128] * weight).reshape(NO, 2, 8, 128))
        spec_s[c] = jnp.concatenate(halves, axis=2).astype(BF)

        @pl.loop(1, NP)
        def _(i):
            spectra_copy(c, (mp + i) % NP).start()

        own_spectra(c).start()

    def forward_copy(c, x):
        return pltpu.make_async_remote_copy(
            src_ref=fwd_s.at[c, x], dst_ref=fwd_r.at[c, mx],
            send_sem=s3.at[c], recv_sem=r3.at[c],
            device_id=(my * NX + x, me), device_id_type=MESH,
        )

    def own_forward(c):
        return pltpu.make_async_copy(fwd_s.at[c, mx], fwd_r.at[c, mx], o3.at[c])

    def forward(c):
        own_spectra(c).wait()
        all_but_one(spec_r.at[c, pl.ds(0, NP - 1)], r2.at[c])
        z = jnp.dot(perm2[...], spec_r[c].reshape(512, 128), preferred_element_type=F32).astype(BF)
        fwd_s[c] = jnp.concatenate([z[:256], z[256:]], axis=1).reshape(NX, 64, TC)

        @pl.loop(1, NX)
        def _(i):
            forward_copy(c, (mx + i) % NX).start()

        own_forward(c).start()

    def analysed(c, lb):
        return lax.dot_general(
            fwd_r[c].reshape(256, TC),
            lv[c, mh, pl.ds(pl.multiple_of(lb * LB, LB), LB), :],
            (((1,), (1,)), ((), ())),
            preferred_element_type=F32,
        )

    def forwarded(c):
        own_forward(c).wait()
        all_but_one(fwd_r.at[c, pl.ds(0, NX - 1)], r3.at[c])

    own_prev.wait()
    all_but_one(fp_r.at[pl.ds(0, NH - 1)], r0)

    for h in range(NH):
        for k in range(2):
            first = (h % NX) * 64 + k * 32 + (h // NX) * 16
            acc[first : first + 16, :] = fp_r[h, 16 * k : 16 * k + 16, :].astype(F32)

    forward(0)

    @pl.loop(1, NC)
    def _(c):
        forward(c)
        forwarded(c - 1)
        for lb in range(NB):
            acc[:, lb * LB : lb * LB + LB] += analysed(c - 1, lb)

    forwarded(NC - 1)

    def result_copy(b, dest):
        return pltpu.make_async_remote_copy(
            src_ref=res_s.at[b, dest],
            dst_ref=out.at[:, mh, :, pl.ds(pl.multiple_of(b * LB, LB), LB)],
            send_sem=s4.at[b], recv_sem=r4.at[b],
            device_id=(dest, me), device_id_type=MESH,
        )

    def own_result(b):
        return pltpu.make_async_copy(
            res_s.at[b, mh], out.at[:, mh, :, pl.ds(pl.multiple_of(b * LB, LB), LB)], o4.at[b]
        )

    @pl.loop(0, NB)
    def _(b):
        lanes = pl.ds(pl.multiple_of(b * LB, LB), LB)
        total = acc[:, lanes] + analysed(NC - 1, b)
        rhs = jnp.concatenate(
            [
                jnp.concatenate(
                    [
                        total[(h % NX) * 64 + k * 32 + (h // NX) * 16 :][:16]
                        for h in range(NH)
                    ],
                    axis=0,
                )
                for k in range(2)
            ],
            axis=1,
        )
        high, low = split(rhs)
        mixed = jnp.dot(
            right_c[...], jnp.concatenate([high, high, low], axis=0), preferred_element_type=F32
        )
        damp = invden[:, lanes]
        high, low = split(mixed * jnp.concatenate([damp, damp], axis=1))
        res = jnp.dot(
            left_c[...], jnp.concatenate([high, high, low], axis=0), preferred_element_type=F32
        ).astype(BF)
        for k in range(2):
            res_s[b, :, k] = res[:, k * LB : k * LB + LB].reshape(NH, RL, LB)

        @pl.loop(1, NH)
        def _(i):
            result_copy(b, (mh + i) % NH).start()

        own_result(b).start()

    all_but_one(fp_s.at[pl.ds(0, NH - 1)], s0)

    @pl.loop(0, NC)
    def _(c):
        all_but_one(sbuf.at[c, :, pl.ds(0, NO - 1)], s1.at[c])
        all_but_one(spec_r.at[c, pl.ds(0, NP - 1)], s2.at[c])
        all_but_one(fwd_s.at[c, pl.ds(0, NX - 1)], s3.at[c])

    @pl.loop(0, NB)
    def _(b):
        all_but_one(res_s.at[b, pl.ds(0, NH - 1)], s4.at[b])
        own_result(b).wait()
        all_but_one(res_s.at[b, pl.ds(0, NH - 1)], r4.at[b])


def body(
    velocity, magnetic, legendre, quad_weight, order_table, field_prev, rates, radial_right, radial_left
):
    hbm = pl.BlockSpec(memory_space=pl.ANY)
    vmem = pl.BlockSpec(memory_space=pltpu.VMEM)
    sem = pltpu.SemaphoreType.DMA
    result = pl.pallas_call(
        kernel,
        out_shape=jax.ShapeDtypeStruct((2, SL, RL, NDEG), BF),
        in_specs=[hbm, hbm, hbm, vmem, vmem, hbm, vmem, vmem, vmem],
        out_specs=hbm,
        scratch_shapes=[
            pltpu.VMEM((4, SL, RL, NDEG), BF),
            pltpu.VMEM((4, SL, RL, NDEG), BF),
            pltpu.VMEM((NC, SL, NDEG, TC), BF),
            pltpu.VMEM((2, SL, RL, NDEG), F32),
            pltpu.VMEM((NH, 32, NDEG), BF),
            pltpu.VMEM((NH, 32, NDEG), BF),
            pltpu.VMEM((4, KK, TC), BF),
            pltpu.VMEM((KK, KK), BF),
            pltpu.VMEM((512, 512), BF),
            pltpu.VMEM((NLON, KK), BF),
            pltpu.VMEM((KK, NLON), BF),
            pltpu.VMEM((NC, 4, NO, 16, TC), BF),
            pltpu.VMEM((NC, 4, NO, 16, TC), BF),
            pltpu.VMEM((NLON, TC), BF),
            pltpu.VMEM((NC, NO, 2, 16, 128), BF),
            pltpu.VMEM((NC, NP, 16, 128), BF),
            pltpu.VMEM((NC, NX, 64, TC), BF),
            pltpu.VMEM((NC, NX, 64, TC), BF),
            pltpu.VMEM((256, NDEG), F32),
            pltpu.VMEM((NB, NH, 2, RL, LB), BF),
            pltpu.VMEM((128, NDEG), F32),
            pltpu.VMEM((128, 384), BF),
            pltpu.VMEM((128, 384), BF),
            sem((2,)),
            sem((NC, SL)),
            sem,
            sem, sem, sem,
            sem((NC,)), sem((NC,)), sem((NC,)),
            sem((NC,)), sem((NC,)), sem((NC,)),
            sem((NC,)), sem((NC,)), sem((NC,)),
            sem((NB,)), sem((NB,)), sem((NB,)),
        ],
        compiler_params=pltpu.CompilerParams(
            collective_id=0, has_side_effects=True, vmem_limit_bytes=58 * 1024 * 1024
        ),
        cost_estimate=pl.CostEstimate(
            flops=18_000_000_000, bytes_accessed=32_000_000, transcendentals=0
        ),
    )(
        velocity.reshape(4, SL, RL, NDEG),
        magnetic.reshape(4, SL, RL, NDEG),
        legendre,
        quad_weight.reshape(NLAT // 128, 128),
        order_table.reshape(1, 128),
        field_prev,
        rates.reshape(1, 128),
        radial_right,
        radial_left,
    )
    return result.astype(F32)


def solution(mesh):
    return jax.shard_map(
        body,
        mesh=mesh,
        in_specs=(
            P(None, None, "order", "shell", None),
            P(None, None, "order", "shell", None),
            P("order", None, None),
            P(),
            P(),
            P(None, "order", "shell", None),
            P(),
            P(),
            P(),
        ),
        out_specs=P(None, "order", "shell", None),
        check_vma=False,
    )
```

time: 103 us -> 86 us (0.83)
  Pallas kernels: 98.9 us -> 82.5 us
  local copies, waits for them, and re-layouts: 3.6 us -> 0 us
  other arithmetic: 0 us -> 2.13 us
    pallas_call x1, Pallas kernels: 98.9 us -> 82.5 us  [body(): pl.pallas_call(kernel, out_shape=jax.ShapeDtypeStruct((2, SL, RL, NDEG),...]
    unnamed x1 -> x0, local copies, waits for them, and re-layouts: 2.31 us -> none
    convert_element_type x0 -> x1, other arithmetic: none -> 2.13 us  [body(): return result.astype(F32)]
    reshape x1 -> x0, local copies, waits for them, and re-layouts: 1.29 us -> none  [body(): quad_weight.reshape(1, NLAT)]
where the time goes in v2:
time: 86 us; the launch traced here: 84.7 us
  Pallas kernels  82.5 us (96%)
  other arithmetic  2.13 us (2%)
    pallas_call x1, Pallas kernels, body(): pl.pallas_call(kernel, out_shape=jax.ShapeDtypeStruct((2, SL, RL, NDEG),...  82.5 us
    convert_element_type x1, other arithmetic, body(): return result.astype(F32)  2.13 us

profile of v2, /device:TPU:0, one launch (start us, length us, event | category | flops | bytes accessed | tf_op | source)
XLA Modules:
  0.0 84.7 jit_solution(8415182581409484163)
XLA Ops:
  0.0 82.5 %shard_map.91 = bf16[2,8,16,1024]{3,2,1,0:T(8,128)(2,1)} custom-call(bf16[4,8,16,1024]{3,2,1,0:T(8,128)(2,1)} %bitcast.5, bf16[4,8,16,1024]{3,2,1,0:T(8,128)(2,1)} %bitcast.6, bf16[8,1024,1536]{2,1,0:T(8,128)(2,1)} %leg.1, f32[12,128]{1,0:T(8,128)} %bitcast.7, s32[1,128]{1,0:T(1,128)} %bitcast.8, f32[2,8,16,1024]{3,2,1,0:T(8,128)} %fprev.1, ...), custom_call_target="tpu_custom_call" | custom-call | flops 17999998976 | bytes 32000000 | tf_op jit(solution)/shard_map/pallas_call | solution.py:360
  82.5 2.1 %convert_element_type.3 = f32[2,8,16,1024]{3,2,1,0:T(8,128)} convert(bf16[2,8,16,1024]{3,2,1,0:T(8,128)(2,1)} %shard_map.91) | non-fusion elementwise | flops 262144 | bytes 1572864 | tf_op jit(solution)/shard_map/convert_element_type | solution.py:415

commit v3 on v2

--- a/solution.py
+++ b/solution.py
@@ -18,7 +18,7 @@
 KK = 256
 TC = 256
 NC = NLAT // TC
-JT = 512
+JT = 1536
 LB = 256
 NB = NDEG // LB
 NP = 2 * NO
@@ -65,6 +65,21 @@
     mx = mh % NX
     mp = my * NO + me
 
+    barrier = pltpu.get_barrier_semaphore()
+
+    @pl.loop(1, NP)
+    def _(i):
+        p = (mp + i) % NP
+        pl.semaphore_signal(
+            barrier, inc=1, device_id=((p // NO) * NX + mx, p % NO), device_id_type=MESH
+        )
+
+    @pl.loop(1, NX)
+    def _(i):
+        x = (mx + i) % NX
+        for y in range(2):
+            pl.semaphore_signal(barrier, inc=1, device_id=(y * NX + x, me), device_id_type=MESH)
+
     def leg_copy(c, s):
         return pltpu.make_async_copy(
             leg.at[s, :, pl.ds(pl.multiple_of(c * TC, TC), TC)], lv.at[c, s], l_sem.at[c, s]
@@ -83,21 +98,6 @@
         def _(s):
             leg_copy(c, s).start()
 
-    barrier = pltpu.get_barrier_semaphore()
-
-    @pl.loop(1, NP)
-    def _(i):
-        p = (mp + i) % NP
-        pl.semaphore_signal(
-            barrier, inc=1, device_id=((p // NO) * NX + mx, p % NO), device_id_type=MESH
-        )
-
-    @pl.loop(1, NX)
-    def _(i):
-        x = (mx + i) % NX
-        for y in range(2):
-            pl.semaphore_signal(barrier, inc=1, device_id=(y * NX + x, me), device_id_type=MESH)
-
     row, col = iota((KK, KK), 0), iota((KK, KK), 1)
     source = slot_of(row) * 32 + part_of(row) * 16 + row // 16
     perm[...] = (col == source).astype(F32).astype(BF)
@@ -112,18 +112,6 @@
         )
 
     own_prev = pltpu.make_async_copy(fp_s.at[mh], fp_r.at[mh], o0)
-    copy_f.wait()
-    for k in range(2):
-        fp_s[:, 16 * k : 16 * k + 16, :] = fp[k].astype(BF)
-    pl.semaphore_wait(barrier, NP - 1 + 2 * (NX - 1))
-
-    @pl.loop(1, NH)
-    def _(i):
-        prev_copy((mh + i) % NH).start()
-
-    own_prev.start()
-    copy_v.wait()
-    copy_m.wait()
 
     def fields_copy(c, dest):
         return pltpu.make_async_remote_copy(
@@ -135,8 +123,7 @@
     def own_fields(c):
         return pltpu.make_async_copy(sbuf.at[c, :, me], rbuf.at[c, :, me], o1.at[c])
 
-    @pl.loop(0, NC)
-    def _(c):
+    def synthesise(c):
         @pl.loop(0, SL)
         def _(s):
             leg_copy(c, s).wait()
@@ -152,11 +139,34 @@
             z = jnp.dot(perm[...], ybuf[f], preferred_element_type=F32).astype(BF)
             sbuf[c, f] = z.reshape(NO, 16, TC)
 
+    def send_fields(c):
         @pl.loop(1, NO)
         def _(i):
             fields_copy(c, (me + i) % NO).start()
 
         own_fields(c).start()
+
+    copy_v.wait()
+    copy_m.wait()
+    synthesise(0)
+    pl.semaphore_wait(barrier, NP - 1 + 2 * (NX - 1))
+    send_fields(0)
+    copy_f.wait()
+    for k in range(2):
+        fp_s[:, 16 * k : 16 * k + 16, :] = fp[k].astype(BF)
+
+    @pl.loop(1, NH)
+    def _(i):
+        prev_copy((mh + i) % NH).start()
+
+    own_prev.start()
+    synthesise(1)
+    send_fields(1)
+    synthesise(2)
+    send_fields(2)
+    synthesise(3)
+    send_fields(3)
+    synthesise(4)
 
     orders = ot[...].astype(F32)
     ra, ca = iota((KK, 128), 0), iota((KK, 128), 1)
@@ -207,11 +217,11 @@
     def own_spectra(c):
         return pltpu.make_async_copy(spec_s.at[c, me, my], spec_r.at[c, mp], o2.at[c])
 
-    @pl.loop(0, NC)
-    def _(c):
+    def wait_fields(c):
         own_fields(c).wait()
         all_but_one(rbuf.at[c, :, pl.ds(0, NO - 1)], r1.at[c])
 
+    def grid_chunk(c):
         @pl.loop(0, NLON // JT)
         def _(j):
             rows = pl.ds(pl.multiple_of(j * JT, JT), JT)
@@ -269,23 +279,50 @@
         own_forward(c).wait()
         all_but_one(fwd_r.at[c, pl.ds(0, NX - 1)], r3.at[c])
 
-    own_prev.wait()
-    all_but_one(fp_r.at[pl.ds(0, NH - 1)], r0)
-
-    for h in range(NH):
-        for k in range(2):
-            first = (h % NX) * 64 + k * 32 + (h // NX) * 16
-            acc[first : first + 16, :] = fp_r[h, 16 * k : 16 * k + 16, :].astype(F32)
-
-    forward(0)
-
-    @pl.loop(1, NC)
+    def analyse(c):
+        forwarded(c)
+        for lb in range(NB):
+            acc[:, lb * LB : lb * LB + LB] += analysed(c, lb)
+
+    @pl.loop(0, NC)
     def _(c):
-        forward(c)
-        forwarded(c - 1)
-        for lb in range(NB):
-            acc[:, lb * LB : lb * LB + LB] += analysed(c - 1, lb)
-
+        wait_fields(c)
+
+        @pl.when(c + 4 < NC)
+        def _():
+            send_fields(c + 4)
+
+        grid_chunk(c)
+
+        @pl.when(c >= 4)
+        def _():
+            forward(c - 4)
+
+        @pl.when(c + 5 < NC)
+        def _():
+            synthesise(c + 5)
+
+        @pl.when(c == 4)
+        def _():
+            own_prev.wait()
+            all_but_one(fp_r.at[pl.ds(0, NH - 1)], r0)
+            for h in range(NH):
+                for k in range(2):
+                    first = (h % NX) * 64 + k * 32 + (h // NX) * 16
+                    acc[first : first + 16, :] = fp_r[h, 16 * k : 16 * k + 16, :].astype(F32)
+
+        @pl.when(c >= 5)
+        def _():
+            analyse(c - 5)
+
+    forward(NC - 4)
+    forward(NC - 3)
+    analyse(NC - 5)
+    forward(NC - 2)
+    analyse(NC - 4)
+    forward(NC - 1)
+    analyse(NC - 3)
+    analyse(NC - 2)
     forwarded(NC - 1)
 
     def result_copy(b, dest):

time: 86 us -> 79.6 us (0.926); the launches traced: 84.7 us -> 79.4 us
  Pallas kernels: 82.5 us -> 77.2 us
    pallas_call x1, Pallas kernels: 82.5 us -> 77.2 us  [body(): pl.pallas_call(kernel, out_shape=jax.ShapeDtypeStruct((2, SL, RL, NDEG),...]
where the time goes in v3:
time: 79.6 us; the launch traced here: 79.4 us
  Pallas kernels  77.2 us (97%)
  other arithmetic  2.13 us (3%)
    pallas_call x1, Pallas kernels, body(): pl.pallas_call(kernel, out_shape=jax.ShapeDtypeStruct((2, SL, RL, NDEG),...  77.2 us
    convert_element_type x1, other arithmetic, body(): return result.astype(F32)  2.13 us

profile of v3, /device:TPU:0, one launch (start us, length us, event | category | flops | bytes accessed | tf_op | source)
XLA Modules:
  0.0 79.4 jit_solution(3397955541808252121)
XLA Ops:
  0.0 77.2 %shard_map.91 = bf16[2,8,16,1024]{3,2,1,0:T(8,128)(2,1)} custom-call(bf16[4,8,16,1024]{3,2,1,0:T(8,128)(2,1)} %bitcast.5, bf16[4,8,16,1024]{3,2,1,0:T(8,128)(2,1)} %bitcast.6, bf16[8,1024,1536]{2,1,0:T(8,128)(2,1)} %leg.1, f32[12,128]{1,0:T(8,128)} %bitcast.7, s32[1,128]{1,0:T(1,128)} %bitcast.8, f32[2,8,16,1024]{3,2,1,0:T(8,128)} %fprev.1, ...), custom_call_target="tpu_custom_call" | custom-call | flops 17999998976 | bytes 32000000 | tf_op jit(solution)/shard_map/pallas_call | solution.py:397
  77.2 2.1 %convert_element_type.3 = f32[2,8,16,1024]{3,2,1,0:T(8,128)} convert(bf16[2,8,16,1024]{3,2,1,0:T(8,128)(2,1)} %shard_map.91) | non-fusion elementwise | flops 262144 | bytes 1572864 | tf_op jit(solution)/shard_map/convert_element_type | solution.py:452
